TPU v7x, 32 devices: a whole 2x2x4 slice. The times are simulated.
32 devices in a mesh: lat: 4 (over y, x), lon: 8 (over z, core).
Axes of the slice: x: 2, y: 2, z: 4, core: 2. Of those that a mesh axis runs over, the one named last changes fastest.
Arguments:
- tokens: bfloat16 [96, 64, 256], P('lat', 'lon'), may hold values from -6 to 6
- cotangent: bfloat16 [96, 64, 256], P('lat', 'lon'), may hold values from -6 to 6
- query_weight: bfloat16 [256, 256], replicated, may hold values from -0.375 to 0.375
- key_weight: bfloat16 [256, 256], replicated, may hold values from -0.375 to 0.375
- value_weight: bfloat16 [256, 256], replicated, may hold values from -0.375 to 0.375
- out_weight: bfloat16 [256, 256], replicated, may hold values from -0.375 to 0.375
- norm_gain: float32 [256], replicated, may hold values from 0.5 to 1.5
- logit_scale: float32 [8], replicated, may hold values from 2 to 10
Outputs:
- output: bfloat16 [96, 64, 256], P('lat', 'lon')
- grad_tokens: bfloat16 [96, 64, 256], P('lat', 'lon')
- grad_query: float32 [256, 256], replicated
- grad_key: float32 [256, 256], replicated
- grad_value: float32 [256, 256], replicated
- grad_out: float32 [256, 256], replicated
- grad_gain: float32 [256], replicated
- grad_scale: float32 [8], replicated
All inputs are finite; a program needn't handle non-finite values.
Results may differ from a plain program's by a relative error of at most 0.012.
The roundings to bfloat16 on the way count: a program that leaves them out, or rounds other values in their place, can miss the bound.
Values may be sent and summed in bfloat16 or wider, within the bound.
A program may use at most 64 MiB of HBM per device.

v0:
```python
import jax
import jax.numpy as jnp
from jax import lax
from jax.sharding import PartitionSpec as P

HEADS = 8
REACH = 6


EPS = 1e-05
FLOOR = 0.5


def padded(block, sides, width):
    for axis, dim in sides:
        count = lax.axis_size(axis)
        forward = [(i, i + 1) for i in range(count - 1)]
        forward.append((count - 1, 0))
        backward = [(target, source) for source, target in forward]
        low = lax.ppermute(
            lax.slice_in_dim(block, block.shape[dim] - width, None, axis=dim), axis, forward
        )
        high = lax.ppermute(lax.slice_in_dim(block, 0, width, axis=dim), axis, backward)
        block = jnp.concatenate([low, block, high], axis=dim)
    return block


def layer_norm(tokens_f, norm_gain):
    center = jnp.mean(tokens_f, axis=-1, keepdims=True)
    shifted = tokens_f - center
    spread = jnp.mean(shifted * shifted, axis=-1, keepdims=True)
    return norm_gain * shifted * lax.rsqrt(spread + EPS)


def head_norm(raw_values):
    grouped = raw_values.reshape(raw_values.shape[:-1] + (HEADS, raw_values.shape[-1] // HEADS))
    mean_square = jnp.mean(grouped * grouped, axis=-1, keepdims=True) + FLOOR
    return (grouped * lax.rsqrt(mean_square)).reshape(raw_values.shape)


def block_height(tile_rows, tile_cols):
    row_limit = max(1, 128 // tile_cols)
    chosen = 1
    for candidate in range(1, tile_rows + 1):
        if tile_rows % candidate == 0 and candidate <= row_limit:
            chosen = candidate
    return chosen


def fold_axis(extended, length, dim_index):
    middle = lax.slice_in_dim(extended, 2 * REACH, 2 * REACH + length, axis=dim_index)
    lower = lax.slice_in_dim(extended, 0, REACH, axis=dim_index)
    upper = lax.slice_in_dim(extended, length + 3 * REACH, length + 4 * REACH, axis=dim_index)
    low_pad = [(0, 0)] * extended.ndim
    high_pad = [(0, 0)] * extended.ndim
    low_pad[dim_index] = (0, length - REACH)
    high_pad[dim_index] = (length - REACH, 0)
    return middle + jnp.pad(lower, low_pad) + jnp.pad(upper, high_pad)


def visibility(top_row, height, tile_cols, first_row, total_rows):
    pad_cols = tile_cols + 2 * REACH
    query_ids = jnp.arange(height * tile_cols, dtype=jnp.int32)
    key_ids = jnp.arange((height + 2 * REACH) * pad_cols, dtype=jnp.int32)
    query_row = top_row + query_ids // tile_cols
    query_col = query_ids % tile_cols
    key_row = top_row + key_ids // pad_cols
    key_col = key_ids % pad_cols
    row_gap = key_row[None, :] - REACH - query_row[:, None]
    col_gap = key_col[None, :] - REACH - query_col[:, None]
    global_row = first_row + key_row - REACH
    inside = (global_row >= 0) & (global_row < total_rows)
    return (jnp.abs(row_gap) <= REACH) & (jnp.abs(col_gap) <= REACH) & inside[None, :]


def attend_block(
    query_block, grad_block, key_window, value_window, visible, logit_scale, head_size
):
    query_count, features = query_block.shape
    key_count = key_window.shape[0]
    contract_last = (((1,), (1,)), ((), ()))
    contract_first = (((0,), (0,)), ((), ()))

    def one_head(head_index, carried):
        attend_acc, query_acc, key_acc, value_acc, scale_acc = carried
        column = head_index * head_size
        query_head = lax.dynamic_slice_in_dim(query_block, column, head_size, 1)
        key_head = lax.dynamic_slice_in_dim(key_window, column, head_size, 1)
        value_head = lax.dynamic_slice_in_dim(value_window, column, head_size, 1)
        grad_head = lax.dynamic_slice_in_dim(grad_block, column, head_size, 1)
        factor = logit_scale[head_index] / head_size
        raw_dots = lax.dot_general(
            query_head, key_head, contract_last, preferred_element_type=jnp.float32
        )
        exp_scores = jnp.where(visible, jnp.exp(raw_dots * factor), 0.0)
        softmax = exp_scores / jnp.sum(exp_scores, axis=1, keepdims=True)
        softmax_bf = softmax.astype(jnp.bfloat16)
        attend_head = jnp.dot(softmax_bf, value_head, preferred_element_type=jnp.float32)
        prob_grad = lax.dot_general(
            grad_head, value_head, contract_last, preferred_element_type=jnp.float32
        )
        score_grad = softmax * (prob_grad - jnp.sum(softmax * prob_grad, axis=1, keepdims=True))
        scale_part = jnp.sum(score_grad * raw_dots) / head_size
        score_grad_bf = score_grad.astype(jnp.bfloat16)
        query_part = jnp.dot(score_grad_bf, key_head, preferred_element_type=jnp.float32) * factor
        key_part = (
            lax.dot_general(
                score_grad_bf, query_head, contract_first, preferred_element_type=jnp.float32
            )
            * factor
        )
        value_part = lax.dot_general(
            softmax_bf, grad_head, contract_first, preferred_element_type=jnp.float32
        )
        attend_acc = lax.dynamic_update_slice_in_dim(attend_acc, attend_head, column, 1)
        query_acc = lax.dynamic_update_slice_in_dim(query_acc, query_part, column, 1)
        key_acc = lax.dynamic_update_slice_in_dim(key_acc, key_part, column, 1)
        value_acc = lax.dynamic_update_slice_in_dim(value_acc, value_part, column, 1)
        scale_acc = scale_acc + jnp.where(jnp.arange(HEADS) == head_index, scale_part, 0.0)
        return (attend_acc, query_acc, key_acc, value_acc, scale_acc)

    query_zeros = jnp.zeros((query_count, features), jnp.float32)
    key_zeros = jnp.zeros((key_count, features), jnp.float32)
    initial = (query_zeros, query_zeros, key_zeros, key_zeros, jnp.zeros((HEADS,), jnp.float32))
    return lax.fori_loop(0, HEADS, one_head, initial)


def local(
    tokens, cotangent, query_weight, key_weight, value_weight, out_weight, norm_gain, logit_scale
):
    tile_rows, tile_cols, features = tokens.shape
    head_size = features // HEADS
    pad_rows = tile_rows + 2 * REACH
    pad_cols = tile_cols + 2 * REACH
    total_rows = tile_rows * lax.axis_size("lat")
    first_row = lax.axis_index("lat") * tile_rows
    highest = lax.Precision.HIGHEST
    tokens_f = tokens.astype(jnp.float32)
    normed = layer_norm(tokens_f, norm_gain).astype(jnp.bfloat16)
    flat_normed = normed.reshape(-1, features)
    query_raw = jnp.dot(flat_normed, query_weight, preferred_element_type=jnp.float32)
    query_unit = head_norm(query_raw).astype(jnp.bfloat16)
    flat_cotangent = cotangent.reshape(-1, features)
    attend_grad = jnp.dot(flat_cotangent, out_weight.T, preferred_element_type=jnp.float32).astype(
        jnp.bfloat16
    )
    key_raw = jnp.dot(flat_normed, key_weight, preferred_element_type=jnp.float32)
    key_unit = head_norm(key_raw).astype(jnp.bfloat16)
    values = jnp.dot(flat_normed, value_weight, preferred_element_type=jnp.float32).astype(
        jnp.bfloat16
    )
    packed = jnp.concatenate([key_unit, values], axis=1).reshape(tile_rows, tile_cols, 2 * features)
    packed_pad = padded(packed, (("lat", 0), ("lon", 1)), REACH).reshape(-1, 2 * features)
    key_flat = packed_pad[:, :features]
    value_flat = packed_pad[:, features:]
    key_pad_grad = jnp.zeros((pad_rows * pad_cols, features), jnp.float32)
    value_pad_grad = jnp.zeros((pad_rows * pad_cols, features), jnp.float32)
    scale_grad = jnp.zeros((HEADS,), jnp.float32)
    attend_parts = []
    query_parts = []
    height = block_height(tile_rows, tile_cols)
    for block_index in range(tile_rows // height):
        top_row = block_index * height
        query_low = top_row * tile_cols
        query_high = query_low + height * tile_cols
        key_low = top_row * pad_cols
        key_high = key_low + (height + 2 * REACH) * pad_cols
        visible = visibility(top_row, height, tile_cols, first_row, total_rows)
        attend_piece, query_piece, key_piece, value_piece, scale_piece = attend_block(
            query_unit[query_low:query_high],
            attend_grad[query_low:query_high],
            key_flat[key_low:key_high],
            value_flat[key_low:key_high],
            visible,
            logit_scale,
            head_size,
        )
        attend_parts.append(attend_piece)
        query_parts.append(query_piece)
        key_pad_grad = key_pad_grad.at[key_low:key_high].add(key_piece)
        value_pad_grad = value_pad_grad.at[key_low:key_high].add(value_piece)
        scale_grad = scale_grad + scale_piece
    attend = jnp.concatenate(attend_parts, axis=0).astype(jnp.bfloat16)
    query_unit_grad = jnp.concatenate(query_parts, axis=0)
    output = (
        tokens_f
        + jnp.dot(attend, out_weight, preferred_element_type=jnp.float32).reshape(
            tile_rows, tile_cols, features
        )
    ).astype(jnp.bfloat16)
    grad_out = jnp.dot(attend.T, flat_cotangent, preferred_element_type=jnp.float32)
    query_grad = jax.vjp(head_norm, query_raw)[1](query_unit_grad)[0]
    normed_f = flat_normed.astype(jnp.float32)
    from_query = jnp.dot(query_grad, query_weight.T.astype(jnp.float32), precision=highest)
    grad_query = jnp.dot(normed_f.T, query_grad, precision=highest)
    grads_pad = jnp.concatenate([key_pad_grad, value_pad_grad], axis=1).reshape(
        pad_rows, pad_cols, 2 * features
    )
    extended = padded(grads_pad, (("lat", 0), ("lon", 1)), REACH)
    owned = fold_axis(fold_axis(extended, tile_rows, 0), tile_cols, 1).reshape(-1, 2 * features)
    key_grad = jax.vjp(head_norm, key_raw)[1](owned[:, :features])[0]
    value_grad = owned[:, features:]
    normed_grad = from_query + jnp.dot(
        key_grad, key_weight.T.astype(jnp.float32), precision=highest
    )
    normed_grad = normed_grad + jnp.dot(
        value_grad, value_weight.T.astype(jnp.float32), precision=highest
    )
    grad_key = jnp.dot(normed_f.T, key_grad, precision=highest)
    grad_value = jnp.dot(normed_f.T, value_grad, precision=highest)
    norm_back = jax.vjp(layer_norm, tokens_f, norm_gain)[1]
    token_grad, gain_grad = norm_back(normed_grad.reshape(tile_rows, tile_cols, features))
    grad_tokens = (cotangent.astype(jnp.float32) + token_grad).astype(jnp.bfloat16)
    summed = lax.psum(
        (grad_query, grad_key, grad_value, grad_out, gain_grad, scale_grad), ("lat", "lon")
    )
    return (output, grad_tokens, summed[0], summed[1], summed[2], summed[3], summed[4], summed[5])


def solution(mesh):
    return jax.shard_map(
        local,
        mesh=mesh,
        in_specs=(P("lat", "lon", None), P("lat", "lon", None), P(), P(), P(), P(), P(), P()),
        out_specs=(P("lat", "lon", None), P("lat", "lon", None), P(), P(), P(), P(), P(), P()),
        check_vma=False,
    )
```

profile of v0, /device:TPU:0, one launch (start us, length us, event | category | flops | bytes accessed | tf_op | source)
XLA Modules:
  0.0 323.9 jit_solution(6768133511206301140)
XLA Ops:
  10.4 1.2 multiply_reduce_fusion.6
  12.5 1.1 convolution_convert_fusion.1
  13.6 3.0 collective-permute-start
  22.7 3.5 %collective-permute-start.3 = (bf16[36,6,512]{2,1,0:T(8,128)(2,1)S(1)}, bf16[36,6,512]{2,1,0:T(8,128)(2,1)S(1)}, u32[]{:S(2)}, u32[]{:S(2)}) collective-permute-start(bf16[36,6,512]{2,1,0:T(8,128)(2,1)S(1)} %get-tuple-element.779), channel_id=1, source_target_pairs={{1,0},{2,1},{3,2},{4,3},{5,4},{6,5},{7,6},{0,7},{9,8},{10,9},{11,1... | collective-permute-start | bytes 663560 | tf_op jit(solution)/shard_map/ppermute | solution.py:23
  26.3 5.0 %collective-permute-done.2 = bf16[36,6,512]{2,1,0:T(8,128)(2,1)S(1)} collective-permute-done((bf16[36,6,512]{2,1,0:T(8,128)(2,1)S(1)}, bf16[36,6,512]{2,1,0:T(8,128)(2,1)S(1)}, u32[]{:S(2)}, u32[]{:S(2)}) %collective-permute-start.2) | collective-permute-done | bytes 221216 | tf_op jit(solution)/shard_map/ppermute | solution.py:20
  33.0 36.9 %while.48 = (s32[]{:T(128)}, bf16[96,256]{0,1:T(8,128)(2,1)S(1)}, f32[96,256]{0,1:T(8,128)S(1)}, f32[480,256]{0,1:T(8,128)S(1)}, f32[480,256]{0,1:T(8,128)S(1)},...) while((s32[]{:T(128)}, bf16[96,256]{0,1:T(8,128)(2,1)S(1)}, ...), condition=%wide.region_8.9_spmd.clone, body=%wide.region_4.8_spmd.clone.sunk | while | flops 19141476 | bytes 2724861 | solution.py:125
  71.5 57.8 %while.49 = (s32[]{:T(128)}, bf16[96,256]{0,1:T(8,128)(2,1)S(1)}, f32[96,256]{0,1:T(8,128)S(1)}, f32[480,256]{0,1:T(8,128)S(1)}, f32[480,256]{0,1:T(8,128)}, /*i...) while((s32[]{:T(128)}, bf16[96,256]{0,1:T(8,128)(2,1)S(1)}, ...), condition=%wide.region_13.14_spmd.clone, body=%wide.region_9.13_spmd.clone.sunk | while | flops 19141476 | bytes 2725621 | solution.py:125
  87.2 1.2 fusion.184
  130.0 2.0 slice_add_fusion
  132.3 3.0 scatter-add.19
  135.4 1.8 scatter-add.15
  138.2 1.1 copy.35
  142.9 1.8 collective-permute-start.5
  151.7 5.3 %collective-permute-done.5 = f32[6,20,512]{2,1,0:T(8,128)} collective-permute-done((f32[6,20,512]{2,1,0:T(8,128)}, f32[6,20,512]{2,1,0:T(8,128)}, u32[]{:S(2)}, u32[]{:S(2)}) %collective-permute-start.5) | collective-permute-done | bytes 245792 | tf_op jit(solution)/shard_map/ppermute | solution.py:23
  159.9 2.9 collective-permute-start.7
  164.7 1.1 fusion.87
  165.8 7.4 %collective-permute-done.6 = f32[48,6,512]{2,0,1:T(8,128)S(1)} collective-permute-done((f32[48,6,512]{2,0,1:T(8,128)S(1)}, f32[48,6,512]{2,0,1:T(8,128)S(1)}, u32[]{:S(2)}, u32[]{:S(2)}) %collective-permute-start.6) | collective-permute-done | bytes 589856 | tf_op jit(solution)/shard_map/ppermute | solution.py:20
  177.8 1.1 fusion.91
  180.0 39.2 %all-reduce.4 = (f32[256]{0:T(256)}, f32[8]{0:T(128)}) all-reduce(f32[256]{0:T(256)S(1)} %get-tuple-element.684, f32[8]{0:T(128)S(1)} %copy-done.42), channel_id=1, replica_groups=mesh['lat'=4,'lon'=8] {'lat','lon'}, use_global_device_ids=true, to_apply=%region_23.24 | all-reduce | flops 264 | bytes 2112 | tf_op jit(solution)/shard_map/psum | solution.py:214
  220.0 90.3 %all-reduce.8.cloned.1.call-done = (f32[256,256]{1,0:T(8,128)}, f32[256,256]{1,0:T(8,128)}, f32[256,256]{1,0:T(8,128)}, f32[256,256]{1,0:T(8,128)}) async-done(((f32[256,256]{1,0:T(8,128)}, f32[256,256]{1,0:T(8,128)}, f32[256,256]{1,0:T(8,128)}, f32[256,256]{1,0:T(8,128)}), (f32[256,256]{1,0:T(8,128)}, f32[256,256]{1,0:T(8,128)}, f32[256,256]{1,0:T(8,128)}, ...) | async-done | bytes 1048592 | tf_op jit(solution)/shard_map/psum | solution.py:214
  310.3 1.7 copy.99
  312.0 1.7 copy.100
  313.7 1.7 copy.101
  315.3 1.7 copy.102
  (322 shorter events, 107.9 us)
Async XLA Ops:
  7.2 11.7 %copy-start.1 = (bf16[24,8,256]{2,1,0:T(8,128)(2,1)S(1)}, bf16[24,8,256]{2,1,0:T(8,128)(2,1)}, u32[]{:S(2)}) copy-start(bf16[24,8,256]{2,1,0:T(8,128)(2,1)} %param.20) | copy-start | bytes 294916
  7.2 11.7 %copy-start.25 = (f32[256]{0:T(256)S(1)}, f32[256]{0:T(256)}, u32[]{:S(2)}) copy-start(f32[256]{0:T(256)} %param.26) | copy-start | bytes 3076
  7.2 11.6 %copy-start.18 = (bf16[256,256]{1,0:T(8,128)(2,1)S(1)}, bf16[256,256]{1,0:T(8,128)(2,1)}, u32[]{:S(2)}) copy-start(bf16[256,256]{1,0:T(8,128)(2,1)} %param.22) | copy-start | bytes 393220
  7.2 303.1 %all-reduce.8.cloned.1.call-start = ((), (), s32[]{:S(2)}) async-start(), calls=%async_computation | async-start | bytes 2097152 | tf_op jit(solution)/shard_map/psum | solution.py:214
  11.6 10.6 %copy-start.6 = (bf16[24,8,256]{2,1,0:T(8,128)(2,1)S(1)}, bf16[24,8,256]{2,1,0:T(8,128)(2,1)}, u32[]{:S(2)}) copy-start(bf16[24,8,256]{2,1,0:T(8,128)(2,1)} %param.21) | copy-start | bytes 294916
  11.7 10.6 %copy-start.21 = (bf16[256,256]{1,0:T(8,128)(2,1)S(1)}, bf16[256,256]{1,0:T(8,128)(2,1)}, u32[]{:S(2)}) copy-start(bf16[256,256]{1,0:T(8,128)(2,1)} %param.25) | copy-start | bytes 393220
  13.6 8.9 %collective-permute-start = (bf16[6,8,512]{2,1,0:T(8,128)(2,1)S(1)}, bf16[6,8,512]{2,1,0:T(8,128)(2,1)S(1)}, u32[]{:S(2)}, u32[]{:S(2)}) collective-permute-start(bf16[6,8,512]{2,1,0:T(8,128)(2,1)S(1)} %get-tuple-element.780), channel_id=1, source_target_pairs={{0,8},{8,16},{16,24},{24,0},{1,9},{9,17},{17,25},{25,1},{2,10},{10... | collective-permute-start | bytes 147464 | tf_op jit(solution)/shard_map/ppermute | solution.py:20
  16.6 5.9 %collective-permute-start.1 = (bf16[6,8,512]{2,1,0:T(8,128)(2,1)S(1)}, bf16[6,8,512]{2,1,0:T(8,128)(2,1)S(1)}, u32[]{:S(2)}, u32[]{:S(2)}) collective-permute-start(bf16[6,8,512]{2,1,0:T(8,128)(2,1)S(1)} %get-tuple-element.781), channel_id=1, source_target_pairs={{8,0},{16,8},{24,16},{0,24},{9,1},{17,9},{25,17},{1,25},{10,2},{18... | collective-permute-start | bytes 147464 | tf_op jit(solution)/shard_map/ppermute | solution.py:23
  22.7 8.6 %collective-permute-start.2 = (bf16[36,6,512]{2,1,0:T(8,128)(2,1)S(1)}, bf16[36,6,512]{2,1,0:T(8,128)(2,1)S(1)}, u32[]{:S(2)}, u32[]{:S(2)}) collective-permute-start(bf16[36,6,512]{2,1,0:T(8,128)(2,1)S(1)} %get-tuple-element.778), channel_id=1, source_target_pairs={{0,1},{1,2},{2,3},{3,4},{4,5},{5,6},{6,7},{7,0},{8,9},{9,10},{10,1... | collective-permute-start | bytes 663560 | tf_op jit(solution)/shard_map/ppermute | solution.py:20
  22.7 8.9 %collective-permute-start.3 = (bf16[36,6,512]{2,1,0:T(8,128)(2,1)S(1)}, bf16[36,6,512]{2,1,0:T(8,128)(2,1)S(1)}, u32[]{:S(2)}, u32[]{:S(2)}) collective-permute-start(bf16[36,6,512]{2,1,0:T(8,128)(2,1)S(1)} %get-tuple-element.779), channel_id=1, source_target_pairs={{1,0},{2,1},{3,2},{4,3},{5,4},{6,5},{7,6},{0,7},{9,8},{10,9},{11,1... | collective-permute-start | bytes 663560 | tf_op jit(solution)/shard_map/ppermute | solution.py:23
  33.0 38.5 %copy-start.10 = (bf16[96,256]{0,1:T(8,128)(2,1)S(1)}, bf16[96,256]{0,1:T(8,128)(2,1)}, u32[]{:S(2)}) copy-start(bf16[96,256]{0,1:T(8,128)(2,1)} %copy-done.9) | copy-start | bytes 147460
  33.0 38.5 %copy-start.31 = (f32[8]{0:T(128)S(1)}, f32[8]{0:T(128)}, u32[]{:S(2)}) copy-start(f32[8]{0:T(128)} %custom-call.1) | copy-start | bytes 100
  33.0 38.5 %copy-start.37 = (s32[480]{0:T(512)S(1)}, s32[480]{0:T(512)}, u32[]{:S(2)}) copy-start(s32[480]{0:T(512)} %get-tuple-element.1038) | copy-start | bytes 5764
  33.0 38.5 %copy-start.41 = (pred[480]{0:T(512)(128)(4,1)S(1)}, pred[480]{0:T(512)(128)(4,1)}, u32[]{:S(2)}) copy-start(pred[480]{0:T(512)(128)(4,1)} %get-tuple-element.1041) | copy-start | bytes 1444
  33.0 38.5 %copy-start.44 = (s32[96]{0:T(128)S(1)}, s32[96]{0:T(128)}, u32[]{:S(2)}) copy-start(s32[96]{0:T(128)} %get-tuple-element.1037) | copy-start | bytes 1156
  138.2 7.7 %copy-start.30 = (f32[192,8]{0,1:T(8,128)S(1)}, f32[192,8]{0,1:T(8,128)}, u32[]{:S(2)}) copy-start(f32[192,8]{0,1:T(8,128)} %copy-done.29) | copy-start | bytes 18436
  138.2 8.4 %copy-start.7 = (bf16[24,8,256]{2,1,0:T(8,128)(2,1)S(1)}, bf16[24,8,256]{2,1,0:T(8,128)(2,1)}, u32[]{:S(2)}) copy-start(bf16[24,8,256]{2,1,0:T(8,128)(2,1)} %param.21) | copy-start | bytes 294916
  138.2 8.4 %copy-start.12 = (bf16[96,256]{0,1:T(8,128)(2,1)S(1)}, bf16[96,256]{0,1:T(8,128)(2,1)}, u32[]{:S(2)}) copy-start(bf16[96,256]{0,1:T(8,128)(2,1)} %copy-done.11) | copy-start | bytes 147460
  138.2 8.4 %copy-start.15 = (bf16[96,256]{0,1:T(8,128)(2,1)S(1)}, bf16[96,256]{0,1:T(8,128)(2,1)}, u32[]{:S(2)}) copy-start(bf16[96,256]{0,1:T(8,128)(2,1)} %copy-done.14) | copy-start | bytes 147460
  140.0 10.5 %collective-permute-start.4 = (f32[6,20,512]{2,1,0:T(8,128)}, f32[6,20,512]{2,1,0:T(8,128)}, u32[]{:S(2)}, u32[]{:S(2)}) collective-permute-start(f32[6,20,512]{2,1,0:T(8,128)} %slice.187), channel_id=1, source_target_pairs={{0,8},{8,16},{16,24},{24,0},{1,9},{9,17},{17,25},{25,1},{2,10},{10... | collective-permute-start | bytes 737288 | tf_op jit(solution)/shard_map/ppermute | solution.py:20
  142.9 14.0 %collective-permute-start.5 = (f32[6,20,512]{2,1,0:T(8,128)}, f32[6,20,512]{2,1,0:T(8,128)}, u32[]{:S(2)}, u32[]{:S(2)}) collective-permute-start(f32[6,20,512]{2,1,0:T(8,128)} %slice.189), channel_id=1, source_target_pairs={{8,0},{16,8},{24,16},{0,24},{9,1},{17,9},{25,17},{1,25},{10,2},{18... | collective-permute-start | bytes 737288 | tf_op jit(solution)/shard_map/ppermute | solution.py:23
  158.6 14.6 %collective-permute-start.6 = (f32[48,6,512]{2,0,1:T(8,128)S(1)}, f32[48,6,512]{2,0,1:T(8,128)S(1)}, u32[]{:S(2)}, u32[]{:S(2)}) collective-permute-start(f32[48,6,512]{2,0,1:T(8,128)S(1)} %copy.38), channel_id=1, source_target_pairs={{0,1},{1,2},{2,3},{3,4},{4,5},{5,6},{6,7},{7,0},{8,9},{9,10},{10,1... | collective-permute-start | bytes 1769480 | tf_op jit(solution)/shard_map/ppermute | solution.py:20
  159.9 14.6 %collective-permute-start.7 = (f32[48,6,512]{2,0,1:T(8,128)S(1)}, f32[48,6,512]{2,0,1:T(8,128)S(1)}, u32[]{:S(2)}, u32[]{:S(2)}) collective-permute-start(f32[48,6,512]{2,0,1:T(8,128)S(1)} %copy.39), channel_id=1, source_target_pairs={{1,0},{2,1},{3,2},{4,3},{5,4},{6,5},{7,6},{0,7},{9,8},{10,9},{11,1... | collective-permute-start | bytes 1769480 | tf_op jit(solution)/shard_map/ppermute | solution.py:23
  177.8 41.4 %copy-start.8 = (bf16[24,8,256]{2,1,0:T(8,128)(2,1)S(1)}, bf16[24,8,256]{2,1,0:T(8,128)(2,1)}, u32[]{:S(2)}) copy-start(bf16[24,8,256]{2,1,0:T(8,128)(2,1)} %param.21) | copy-start | bytes 294916
  (30 other events, 75.5 us)
Sparse Core Ops, SparseCore 0:
  179.8 130.4 all-reduce.7
where the time goes:
time: 326 us; the launch traced here: 324 us
  waiting for transfers between devices  109 us (33%)
  matrix products  59.8 us (18%)
  blocking collectives  39.2 us (12%)
  local copies, waits for them, and re-layouts  36.5 us (11%)
  other arithmetic  27.6 us (8%)
  loops' own time  22.1 us (7%)
  between operations  15 us (5%)
  starting transfers between devices  14.4 us (4%)
    psum x1, waiting for transfers between devices, local(): lax.psum((grad_query, grad_key, grad_value, grad_out, gain_grad, scale_gr...  90.3 us
    psum x1, blocking collectives, local(): lax.psum((grad_query, grad_key, grad_value, grad_out, gain_grad, scale_gr...  39.2 us
    another operation x2, loops' own time, attend_block(): return lax.fori_loop(0, HEADS, one_head, initial)  22.1 us
    reduce_sum x16, other arithmetic, one_head(): scale_part = jnp.sum(score_grad * raw_dots) / head_size  12.5 us
    unnamed x98, local copies, waits for them, and re-layouts  12.4 us
    ppermute x4, waiting for transfers between devices, padded(): lax.ppermute(lax.slice_in_dim(block, block.shape[dim] - width, None, axis...  12.4 us
    dot_general x16, matrix products, one_head(): lax.dot_general(query_head, key_head, contract_last, preferred_element_ty...  12.2 us
    dot_general x16, matrix products, one_head(): lax.dot_general(grad_head, value_head, contract_last, preferred_element_t...  12.1 us
  transfers between devices with their start and end apart: 9, of which 6 were waited for; matrix products, arithmetic and copies ran while one was open for 5% of the time, Pallas kernels for 0%

commit v1 on v0

v1 whole, which is shorter than its diff:
```python
import functools

import jax
import jax.numpy as jnp
from jax import lax
from jax.experimental import pallas as pl
from jax.experimental.pallas import tpu as pltpu
from jax.sharding import PartitionSpec as P

HEADS = 8
REACH = 6
EPS = 1e-05
FLOOR = 0.5
BLOCK = 8
MESH = pl.DeviceIdType.MESH
F32 = jnp.float32
BF16 = jnp.bfloat16
OFFSETS = ((0, -1), (0, 1), (-1, 0), (1, 0), (-1, -1), (-1, 1), (1, -1), (1, 1))


def dot_nn(a, b):
    return lax.dot_general(a, b, (((1,), (0,)), ((), ())), preferred_element_type=F32)


def dot_nt(a, b):
    return lax.dot_general(a, b, (((1,), (1,)), ((), ())), preferred_element_type=F32)


def dot_tn(a, b):
    return lax.dot_general(a, b, (((0,), (0,)), ((), ())), preferred_element_type=F32)


def group_mean(x, ones):
    high = x.astype(BF16)
    low = (x - high.astype(F32)).astype(BF16)
    return dot_nn(high, ones) + dot_nn(low, ones)


def kernel(
    dims,
    tok, cot, wq, wk, wv, wo, gain, wide, scale,
    out, gtok, fin_out, small_out,
    win, kbuf, vbuf, kraw, nrm, qu, qraw, ag, qe, ge, sc, dp, pb, db, dk, dv, dq, att,
    wg, ngs, ngo, rback, rcore, s1, rlat, s2, rz, fin, small, smcore, smlat, smz,
    hs, hr, bs, br, cs, cr, ls, lr, zs, zr, gs, gr,
):
    n_lat, n_lon, rows, cols = dims
    nz = n_lon // 2
    count = rows * cols
    halo = REACH * cols
    tall = count + 2 * halo
    feats = tok.shape[1]
    head = feats // HEADS
    nb = BLOCK * cols
    wrows = (BLOCK + 2 * REACH) * cols
    keys = 3 * wrows
    reduce_here = wg.shape[0] % (2 * n_lat * nz * 16) == 0
    a = lax.axis_index("lat")
    b = lax.axis_index("lon")
    core = lax.rem(b, 2)
    z = b // 2
    sibling = (a, b + 1 - 2 * core)

    def lat_peer(j):
        return (lax.rem(a + j, n_lat), b)

    def z_peer(j):
        return (a, lax.rem(z + j, nz) * 2 + core)

    def near(da, db):
        return (lax.rem(a + da + n_lat, n_lat), lax.rem(b + db + n_lon, n_lon))

    peers = [near(*o) for o in OFFSETS]
    if reduce_here:
        peers += [sibling] + [lat_peer(j) for j in range(1, n_lat)] + [z_peer(j) for j in range(1, nz)]
    barrier = pltpu.get_barrier_semaphore()
    for p in peers:
        pl.semaphore_signal(barrier, inc=1, device_id=p, device_id_type=MESH)
    pl.semaphore_wait(barrier, len(peers))

    def send(src, dst, s, r, to):
        c = pltpu.make_async_remote_copy(
            src_ref=src, dst_ref=dst, send_sem=s, recv_sem=r, device_id=to, device_id_type=MESH
        )
        c.start()
        return c

    def strip(da):
        return {0: (0, halo, count), 1: (count - halo, 0, halo), -1: (0, halo + count, halo)}[da]

    halos = []
    for i, (da, d) in enumerate(OFFSETS):
        src, dst, n = strip(da)
        halos.append(
            send(
                tok.at[pl.ds(src, n)], win.at[pl.ds((1 - d) * tall + dst, n)],
                hs.at[i], hr.at[i], near(da, d),
            )
        )

    lane = lax.broadcasted_iota(jnp.int32, (1, feats), 1) // head
    gi = lax.broadcasted_iota(jnp.int32, (feats, feats), 0) // head
    gj = lax.broadcasted_iota(jnp.int32, (feats, feats), 1) // head
    ones = jnp.where(gi == gj, 1.0 / head, 0.0).astype(BF16)

    def norm_parts(x):
        x = x.astype(F32)
        sh = x - jnp.mean(x, axis=-1, keepdims=True)
        rstd = lax.rsqrt(jnp.mean(sh * sh, axis=-1, keepdims=True) + EPS)
        return sh, rstd

    def project(x, lo, n):
        sh, rstd = norm_parts(x)
        nn = (gain[...] * sh * rstd).astype(BF16)
        nrm[pl.ds(lo, n)] = nn
        kr = dot_nn(nn, wk[...])
        kraw[pl.ds(lo, n)] = kr
        kbuf[pl.ds(lo, n)] = (kr * lax.rsqrt(group_mean(kr * kr, ones) + FLOOR)).astype(BF16)
        vbuf[pl.ds(lo, n)] = dot_nn(nn, wv[...]).astype(BF16)

    mine = tall + halo
    project(tok[...], mine, count)
    qr = dot_nn(nrm[pl.ds(mine, count)], wq[...])
    qraw[...] = qr
    qu[...] = (qr * lax.rsqrt(group_mean(qr * qr, ones) + FLOOR)).astype(BF16)
    ag[...] = dot_nt(cot[...], wo[...]).astype(BF16)
    dk[...] = jnp.zeros_like(dk)
    dv[...] = jnp.zeros_like(dv)
    small[...] = jnp.zeros_like(small)
    for c in halos:
        c.wait()
    project(win[pl.ds(0, tall)], 0, tall)
    project(win[pl.ds(2 * tall, tall)], 2 * tall, tall)
    project(win[pl.ds(tall, halo)], tall, halo)
    project(win[pl.ds(tall + halo + count, halo)], tall + halo + count, halo)

    total_rows = n_lat * rows
    qi = lax.broadcasted_iota(jnp.int32, (nb, keys), 0)
    ki = lax.broadcasted_iota(jnp.int32, (nb, keys), 1)
    tile = (ki >= wrows).astype(jnp.int32) + (ki >= 2 * wrows).astype(jnp.int32)
    within = ki - tile * wrows
    row_gap = within // cols - REACH - qi // cols
    col_gap = lax.rem(within, cols) + tile * cols - cols - lax.rem(qi, cols)
    close = (jnp.abs(row_gap) <= REACH) & (jnp.abs(col_gap) <= REACH)
    krow = within // cols - REACH + a * rows

    def block(i, carried):
        q0 = pl.multiple_of(i * nb, nb)
        qb = qu[pl.ds(q0, nb)]
        gb = ag[pl.ds(q0, nb)]
        for h in range(HEADS):
            qe[pl.ds(h * nb, nb)] = jnp.where(lane == h, qb, jnp.zeros_like(qb))
            ge[pl.ds(h * nb, nb)] = jnp.where(lane == h, gb, jnp.zeros_like(gb))
        starts = [pl.multiple_of(t * tall + i * nb, 16) for t in range(3)]
        kw = jnp.concatenate([kbuf[pl.ds(s, wrows)] for s in starts], axis=0)
        vw = jnp.concatenate([vbuf[pl.ds(s, wrows)] for s in starts], axis=0)
        sc[...] = dot_nt(qe[...], kw)
        dp[...] = dot_nt(ge[...], vw)
        gr_row = krow + i * BLOCK
        seen = jnp.where(close & (gr_row >= 0) & (gr_row < total_rows), 1.0, 0.0)
        for h in range(HEADS):
            part = pl.ds(h * nb, nb)
            s = sc[part]
            e = jnp.exp(s * scale[h]) * seen
            p = e * (1.0 / jnp.sum(e, axis=1, keepdims=True))
            pb[part] = p.astype(BF16)
            t = dp[part]
            g = p * (t - jnp.sum(p * t, axis=1, keepdims=True))
            db[part] = g.astype(BF16)
            tot = jnp.sum(jnp.sum(g * s, axis=1, keepdims=True), axis=0, keepdims=True)
            small[1:2, :] = small[1:2, :] + jnp.where(lane == h, tot * (1.0 / head), 0.0)
        o = dot_nn(pb[...], vw)
        u = dot_nn(db[...], kw)
        oa = jnp.zeros((nb, feats), F32)
        ua = jnp.zeros((nb, feats), F32)
        for h in range(HEADS):
            oa = jnp.where(lane == h, o[h * nb : (h + 1) * nb], oa)
            ua = jnp.where(lane == h, u[h * nb : (h + 1) * nb], ua)
        att[pl.ds(q0, nb)] = oa.astype(BF16)
        dq[pl.ds(q0, nb)] = ua
        kg = dot_tn(db[...], qe[...])
        vg = dot_tn(pb[...], ge[...])
        for t in range(3):
            part = pl.ds(starts[t], wrows)
            dk[part] = dk[part] + kg[t * wrows : (t + 1) * wrows]
            dv[part] = dv[part] + vg[t * wrows : (t + 1) * wrows]
        return carried

    lax.fori_loop(0, rows // BLOCK, block, 0)

    def head_back(raw, g):
        s = lax.rsqrt(group_mean(raw * raw, ones) + FLOOR)
        return s * g - raw * (s * s * s) * group_mean(g * raw, ones)

    dqr = head_back(qraw[...], dq[...] * wide[...]).astype(BF16)
    dkr = head_back(kraw[...], dk[...] * wide[...]).astype(BF16)
    dvb = dv[...].astype(BF16)
    wg[pl.ds(0, feats)] = dot_tn(nrm[pl.ds(mine, count)], dqr).astype(BF16)
    wg[pl.ds(feats, feats)] = dot_tn(nrm[...], dkr).astype(BF16)
    wg[pl.ds(2 * feats, feats)] = dot_tn(nrm[...], dvb).astype(BF16)
    wg[pl.ds(3 * feats, feats)] = dot_tn(att[...], cot[...]).astype(BF16)
    pending = []
    if reduce_here:
        half = wg.shape[0] // 2
        quarter = half // n_lat
        last = quarter // nz
        my_half = pl.multiple_of(core * half, 16)
        other = pl.multiple_of((1 - core) * half, 16)
        c_core = send(wg.at[pl.ds(other, half)], rcore, cs.at[0], cr.at[0], sibling)

    ng = dot_nt(dkr, wk[...]) + dot_nt(dvb, wv[...])
    ngs[...] = ng.astype(BF16)
    backs = []
    for i, (da, d) in enumerate(OFFSETS):
        _, _, n = strip(da)
        src = {0: halo, -1: 0, 1: halo + count}[da]
        backs.append(
            send(
                ngs.at[pl.ds((1 + d) * tall + src, n)], rback.at[i, pl.ds(0, n)],
                bs.at[i], br.at[i], near(da, d),
            )
        )
    own = ng[mine : mine + count] + dot_nt(dqr, wq[...])
    ngo[...] = own
    gsum = jnp.zeros((1, feats), F32)
    for lo, n in ((0, tall), (2 * tall, tall), (tall, halo), (mine + count, halo)):
        sh, rstd = norm_parts(win[pl.ds(lo, n)])
        gsum = gsum + jnp.sum(ng[lo : lo + n] * (sh * rstd), axis=0, keepdims=True)
    sh, rstd = norm_parts(tok[...])
    gsum = gsum + jnp.sum(own * (sh * rstd), axis=0, keepdims=True)
    small[0:1, :] = gsum

    if reduce_here:
        m_core = send(small, smcore, cs.at[1], cr.at[1], sibling)
        c_core.wait()
        s1[...] = (wg[pl.ds(my_half, half)].astype(F32) + rcore[...].astype(F32)).astype(BF16)
        c_lat = []
        for j in range(1, n_lat):
            to = lat_peer(j)
            lo = pl.multiple_of(to[0] * quarter, 16)
            c_lat.append(send(s1.at[pl.ds(lo, quarter)], rlat.at[j - 1], ls.at[j], lr.at[j], to))
        m_core.wait()
        smlat[pl.ds(a, 1)] = (small[...] + smcore[...])[None]
        m_lat = [
            send(smlat.at[a], smlat.at[a], ls.at[n_lat + j], lr.at[n_lat + j], lat_peer(j))
            for j in range(1, n_lat)
        ]

    out[...] = (tok[...].astype(F32) + dot_nn(att[...], wo[...])).astype(BF16)
    for c in backs:
        c.wait()
    ngo[...] = ngo[...] + rback[0].astype(F32) + rback[1].astype(F32)
    for da, lo in ((-1, 0), (1, count - halo)):
        part = pl.ds(lo, halo)
        add = ngo[part]
        for i, o in enumerate(OFFSETS):
            if o[0] == -da:
                add = add + rback[i, pl.ds(0, halo)].astype(F32)
        ngo[part] = add
    sh, rstd = norm_parts(tok[...])
    xhat = sh * rstd
    g = ngo[...] * gain[...]
    tg = rstd * (
        g - jnp.mean(g, axis=-1, keepdims=True) - xhat * jnp.mean(g * xhat, axis=-1, keepdims=True)
    )
    gtok[...] = (cot[...].astype(F32) + tg).astype(BF16)

    if reduce_here:
        for c in c_lat:
            c.wait()
        acc = s1[pl.ds(pl.multiple_of(a * quarter, 16), quarter)].astype(F32)
        for j in range(1, n_lat):
            acc = acc + rlat[j - 1].astype(F32)
        s2[...] = acc.astype(BF16)
        c_z = []
        for j in range(1, nz):
            to = z_peer(j)
            lo = pl.multiple_of((to[1] // 2) * last, 16)
            c_z.append(send(s2.at[pl.ds(lo, last)], rz.at[j - 1], zs.at[j], zr.at[j], to))
        for c in m_lat:
            c.wait()
        acc = smlat[0]
        for j in range(1, n_lat):
            acc = acc + smlat[j]
        smz[pl.ds(z, 1)] = acc[None]
        m_z = [
            send(smz.at[z], smz.at[z], zs.at[nz + j], zr.at[nz + j], z_peer(j)) for j in range(1, nz)
        ]
        for c in c_z:
            c.wait()
        acc = s2[pl.ds(pl.multiple_of(z * last, 16), last)].astype(F32)
        for j in range(1, nz):
            acc = acc + rz[j - 1].astype(F32)
        block_lo = pl.multiple_of(my_half + a * quarter, 16)
        leaf = pl.ds(pl.multiple_of(block_lo + z * last, 16), last)
        fin[leaf] = acc.astype(BF16)
        c_z = [send(fin.at[leaf], fin.at[leaf], gs.at[j], gr.at[j], z_peer(j)) for j in range(1, nz)]
        for c in m_z:
            c.wait()
        acc = smz[0]
        for j in range(1, nz):
            acc = acc + smz[j]
        small_out[...] = acc
        for c in c_z:
            c.wait()
        mid = pl.ds(block_lo, quarter)
        c_lat = [
            send(fin.at[mid], fin.at[mid], gs.at[nz + j], gr.at[nz + j], lat_peer(j))
            for j in range(1, n_lat)
        ]
        for c in c_lat:
            c.wait()
        top = pl.ds(my_half, half)
        send(fin.at[top], fin.at[top], gs.at[0], gr.at[0], sibling).wait()
        fin_out[...] = fin[...]
    else:
        fin_out[...] = wg[...]
        small_out[...] = small[...]


def local(dims, tokens, cotangent, wq, wk, wv, wo, norm_gain, logit_scale):
    n_lat, n_lon, rows, cols = dims
    nz = n_lon // 2
    feats = tokens.shape[-1]
    head = feats // HEADS
    count = rows * cols
    halo = REACH * cols
    window = 3 * (count + 2 * halo)
    nb = BLOCK * cols * HEADS
    keys = 3 * (BLOCK + 2 * REACH) * cols
    reduce_here = 4 * feats % (2 * n_lat * nz * 16) == 0
    half = 2 * feats
    quarter = max(16, half // n_lat) if reduce_here else 16
    last = quarter // nz if reduce_here else 16
    pl_lat = n_lat if reduce_here else 2
    pl_z = nz if reduce_here else 2
    vm = pl.BlockSpec(memory_space=pltpu.VMEM)
    sm = pl.BlockSpec(memory_space=pltpu.SMEM)
    dma = pltpu.SemaphoreType.DMA
    factor = logit_scale / head
    V = pltpu.VMEM
    scratch = [
        V((window, feats), BF16), V((window, feats), BF16), V((window, feats), BF16),
        V((window, feats), F32), V((window, feats), BF16),
        V((count, feats), BF16), V((count, feats), F32), V((count, feats), BF16),
        V((nb, feats), BF16), V((nb, feats), BF16),
        V((nb, keys), F32), V((nb, keys), F32), V((nb, keys), BF16), V((nb, keys), BF16),
        V((window, feats), F32), V((window, feats), F32), V((count, feats), F32),
        V((count, feats), BF16),
        V((4 * feats, feats), BF16), V((window, feats), BF16), V((count, feats), F32),
        V((8, count, feats), BF16),
        V((half, feats), BF16), V((half, feats), BF16),
        V((pl_lat - 1, quarter, feats), BF16), V((quarter, feats), BF16),
        V((pl_z - 1, last, feats), BF16), V((4 * feats, feats), BF16),
        V((8, feats), F32), V((8, feats), F32), V((pl_lat, 8, feats), F32), V((pl_z, 8, feats), F32),
        dma((8,)), dma((8,)), dma((8,)), dma((8,)), dma((2,)), dma((2,)),
        dma((2 * pl_lat,)), dma((2 * pl_lat,)), dma((2 * pl_z,)), dma((2 * pl_z,)),
        dma((pl_lat + pl_z,)), dma((pl_lat + pl_z,)),
    ]
    out, gtok, fin, small = pl.pallas_call(
        functools.partial(kernel, dims),
        out_shape=[
            jax.ShapeDtypeStruct((count, feats), BF16),
            jax.ShapeDtypeStruct((count, feats), BF16),
            jax.ShapeDtypeStruct((4 * feats, feats), BF16),
            jax.ShapeDtypeStruct((8, feats), F32),
        ],
        in_specs=[vm] * 8 + [sm],
        out_specs=[vm] * 4,
        scratch_shapes=scratch,
        compiler_params=pltpu.CompilerParams(
            collective_id=0, has_side_effects=True, vmem_limit_bytes=50 * 1024 * 1024
        ),
    )(
        tokens.reshape(count, feats), cotangent.reshape(count, feats), wq, wk, wv, wo,
        norm_gain.reshape(1, feats), jnp.repeat(factor, head).reshape(1, feats), factor,
    )
    fin = fin.astype(F32)
    if not reduce_here:
        fin, small = lax.psum((fin, small), ("lat", "lon"))
    return (
        out.reshape(rows, cols, feats), gtok.reshape(rows, cols, feats),
        fin[:feats], fin[feats : 2 * feats], fin[2 * feats : 3 * feats], fin[3 * feats :],
        small[0], small[1, ::head],
    )


def solution(mesh):
    n_lat, n_lon = mesh.shape["lat"], mesh.shape["lon"]

    def run(tokens, *rest):
        dims = (n_lat, n_lon, tokens.shape[0], tokens.shape[1])
        return local(dims, tokens, *rest)

    return jax.shard_map(
        run,
        mesh=mesh,
        in_specs=(P("lat", "lon", None), P("lat", "lon", None), P(), P(), P(), P(), P(), P()),
        out_specs=(P("lat", "lon", None), P("lat", "lon", None), P(), P(), P(), P(), P(), P()),
        check_vma=False,
    )
```

time: 326 us -> 52.4 us (0.16)
  waiting for transfers between devices: 109 us -> 0 us
  matrix products: 59.8 us -> 0 us
  Pallas kernels: 0 us -> 41.2 us
  blocking collectives: 39.2 us -> 0 us
  other arithmetic: 27.6 us -> 0.01 us
  local copies, waits for them, and re-layouts: 36.5 us -> 10.2 us
  loops' own time: 22.1 us -> 0 us
  starting transfers between devices: 14.4 us -> 0 us
  between operations: 15 us -> 0.66 us
    psum x1 -> x0, waiting for transfers between devices: 90.3 us -> none  [local(): lax.psum((grad_query, grad_key, grad_value, grad_out, gain_grad, scale_gr...]
    dot_general x108 -> x0, matrix products: 59.8 us -> none  [the longest x16 12.2 us: one_head(): lax.dot_general(query_head, key_head, contract_last, preferred_element_ty...]
    pallas_call x0 -> x1, Pallas kernels: none -> 41.2 us  [local(): pl.pallas_call(functools.partial(kernel, dims), out_shape=[jax.ShapeDtype...]
    psum x1 -> x0, blocking collectives: 39.2 us -> none  [local(): lax.psum((grad_query, grad_key, grad_value, grad_out, gain_grad, scale_gr...]
    another operation x2 -> x0, loops' own time: 22.1 us -> none  [attend_block(): return lax.fori_loop(0, HEADS, one_head, initial)]
    ppermute x8 -> x0, waiting for transfers between devices: 18.9 us -> none  [the longest x4 12.4 us: padded(): lax.ppermute(lax.slice_in_dim(block, block.shape[dim] - width, None, axis...]
    reduce_sum x21 -> x0, other arithmetic: 16 us -> none  [the longest x16 12.5 us: one_head(): scale_part = jnp.sum(score_grad * raw_dots) / head_size]
    ppermute x8 -> x0, starting transfers between devices: 14.3 us -> none  [the longest x4 9.32 us: padded(): lax.ppermute(lax.slice_in_dim(block, 0, width, axis=dim), axis, backward)]
  transfers between devices with their start and end apart: 9 -> 0, of which waited for: 6 -> 0; matrix products, arithmetic and copies ran while one was open for 5% -> 0% of each run, Pallas kernels for 0% -> 0%
where the time goes in v1:
time: 52.4 us; the launch traced here: 52.1 us
  Pallas kernels  41.2 us (79%)
  local copies, waits for them, and re-layouts  10.2 us (19%)
  between operations  0.66 us (1%)
    pallas_call x1, Pallas kernels, local(): pl.pallas_call(functools.partial(kernel, dims), out_shape=[jax.ShapeDtype...  41.2 us
    unnamed x18, local copies, waits for them, and re-layouts  7.93 us

profile of v1, /device:TPU:0, one launch (start us, length us, event | category | flops | bytes accessed | tf_op | source)
XLA Modules:
  0.0 52.1 jit_solution(153948382000313971)
XLA Ops:
  0.6 0.0 copy-start.7
  0.6 0.6 %copy-done.7 = f32[8]{0:T(128)S(1)} copy-done((f32[8]{0:T(128)S(1)}, f32[8]{0:T(128)}, u32[]{:S(2)}) %copy-start.7) | copy-done | bytes 56
  1.3 0.1 broadcast_in_dim.3
  1.4 0.0 copy-start.6
  1.4 0.1 reshape_reshape.3.wide
  1.4 0.6 %copy-done.6 = f32[256]{0:T(256)S(1)} copy-done((f32[256]{0:T(256)S(1)}, f32[256]{0:T(256)}, u32[]{:S(2)}) %copy-start.6) | copy-done | bytes 1048
  2.0 0.0 copy-start
  2.0 0.9 %copy-done = bf16[256,256]{1,0:T(8,128)(2,1)S(1)} copy-done((bf16[256,256]{1,0:T(8,128)(2,1)S(1)}, bf16[256,256]{1,0:T(8,128)(2,1)}, u32[]{:S(2)}) %copy-start) | copy-done | bytes 131096
  2.9 0.0 copy-start.1
  3.0 0.9 %copy-done.1 = bf16[256,256]{1,0:T(8,128)(2,1)S(1)} copy-done((bf16[256,256]{1,0:T(8,128)(2,1)S(1)}, bf16[256,256]{1,0:T(8,128)(2,1)}, u32[]{:S(2)}) %copy-start.1) | copy-done | bytes 131096
  3.9 0.0 copy-start.2
  3.9 0.9 %copy-done.2 = bf16[256,256]{1,0:T(8,128)(2,1)S(1)} copy-done((bf16[256,256]{1,0:T(8,128)(2,1)S(1)}, bf16[256,256]{1,0:T(8,128)(2,1)}, u32[]{:S(2)}) %copy-start.2) | copy-done | bytes 131096
  4.8 0.0 copy-start.3
  4.8 0.9 %copy-done.3 = bf16[256,256]{1,0:T(8,128)(2,1)S(1)} copy-done((bf16[256,256]{1,0:T(8,128)(2,1)S(1)}, bf16[256,256]{1,0:T(8,128)(2,1)}, u32[]{:S(2)}) %copy-start.3) | copy-done | bytes 131096
  5.7 0.0 copy-start.4
  5.7 0.9 %copy-done.4 = bf16[24,8,256]{2,1,0:T(8,128)(2,1)S(1)} copy-done((bf16[24,8,256]{2,1,0:T(8,128)(2,1)S(1)}, bf16[24,8,256]{2,1,0:T(8,128)(2,1)}, u32[]{:S(2)}) %copy-start.4) | copy-done | bytes 98328
  6.6 0.0 copy-start.5
  6.6 0.9 %copy-done.5 = bf16[24,8,256]{2,1,0:T(8,128)(2,1)S(1)} copy-done((bf16[24,8,256]{2,1,0:T(8,128)(2,1)S(1)}, bf16[24,8,256]{2,1,0:T(8,128)(2,1)}, u32[]{:S(2)}) %copy-start.5) | copy-done | bytes 98328
  7.5 41.2 %shard_map.143 = (bf16[192,256]{1,0:T(8,128)(2,1)S(1)}, bf16[192,256]{1,0:T(8,128)(2,1)S(1)}, bf16[1024,256]{1,0:T(8,128)(2,1)S(1)}, f32[8,256]{1,0:T(8,128)S(1)}) custom-call(bf16[192,256]{1,0:T(8,128)(2,1)S(1)} %bitcast.7, bf16[192,256]{1,0:T(8,128)(2,1)S(1)} %bitcast.8, bf16[256,256]{1,0:T(8,128)(2,1)S(1)} %copy-done, bf16[256,256]{1,0:T(8,128)(2,1)S(1)} %copy-done.1, ...), custom_call_target="tpu_custom_call" | custom-call | tf_op jit(solution)/shard_map/pallas_call | solution.py:360
  48.7 0.6 %slice.23 = f32[1,8]{1,0:T(1,128)} slice(f32[8,256]{1,0:T(8,128)S(1)} %get-tuple-element.15), slice={[1:2:1], [0:256:32]} | slice | bytes 64 | tf_op jit(solution)/shard_map/slice | solution.py:384
  49.3 0.6 %slice.22 = f32[1,256]{1,0:T(1,128)} slice(f32[8,256]{1,0:T(8,128)S(1)} %get-tuple-element.15), slice={[0:1], [0:256]} | slice | bytes 2048 | tf_op jit(solution)/shard_map/slice | solution.py:384
  49.8 1.0 %fusion = (f32[256,256]{1,0:T(8,128)}, f32[256,256]{1,0:T(8,128)}, f32[256,256]{1,0:T(8,128)}, f32[256,256]{1,0:T(8,128)}) fusion(bf16[1024,256]{1,0:T(8,128)(2,1)S(1)} %get-tuple-element.14), kind=kLoop, calls=%fused_computation.1 | loop fusion | bytes 2097152 | tf_op jit(solution)/shard_map/slice | solution.py:383
  50.8 0.6 %copy.18 = bf16[24,8,256]{2,1,0:T(8,128)(2,1)} copy(bf16[24,8,256]{2,1,0:T(8,128)(2,1)S(1)} %bitcast.10) | data formatting | bytes 196608
  51.4 0.6 %copy.19 = bf16[24,8,256]{2,1,0:T(8,128)(2,1)} copy(bf16[24,8,256]{2,1,0:T(8,128)(2,1)S(1)} %bitcast.9) | data formatting | bytes 196608
  (1 shorter events, 0.0 us)
Async XLA Ops:
  0.6 0.7 %copy-start.7 = (f32[8]{0:T(128)S(1)}, f32[8]{0:T(128)}, u32[]{:S(2)}) copy-start(f32[8]{0:T(128)} %param.15) | copy-start | bytes 100
  1.4 0.7 %copy-start.6 = (f32[256]{0:T(256)S(1)}, f32[256]{0:T(256)}, u32[]{:S(2)}) copy-start(f32[256]{0:T(256)} %param.14) | copy-start | bytes 3076
  2.0 0.9 %copy-start = (bf16[256,256]{1,0:T(8,128)(2,1)S(1)}, bf16[256,256]{1,0:T(8,128)(2,1)}, u32[]{:S(2)}) copy-start(bf16[256,256]{1,0:T(8,128)(2,1)} %wq.1) | copy-start | bytes 393220
  2.9 0.9 %copy-start.1 = (bf16[256,256]{1,0:T(8,128)(2,1)S(1)}, bf16[256,256]{1,0:T(8,128)(2,1)}, u32[]{:S(2)}) copy-start(bf16[256,256]{1,0:T(8,128)(2,1)} %wk.1) | copy-start | bytes 393220
  3.9 0.9 %copy-start.2 = (bf16[256,256]{1,0:T(8,128)(2,1)S(1)}, bf16[256,256]{1,0:T(8,128)(2,1)}, u32[]{:S(2)}) copy-start(bf16[256,256]{1,0:T(8,128)(2,1)} %wv.1) | copy-start | bytes 393220
  4.8 0.9 %copy-start.3 = (bf16[256,256]{1,0:T(8,128)(2,1)S(1)}, bf16[256,256]{1,0:T(8,128)(2,1)}, u32[]{:S(2)}) copy-start(bf16[256,256]{1,0:T(8,128)(2,1)} %wo.1) | copy-start | bytes 393220
  5.7 0.9 %copy-start.4 = (bf16[24,8,256]{2,1,0:T(8,128)(2,1)S(1)}, bf16[24,8,256]{2,1,0:T(8,128)(2,1)}, u32[]{:S(2)}) copy-start(bf16[24,8,256]{2,1,0:T(8,128)(2,1)} %param.8) | copy-start | bytes 294916
  6.6 0.9 %copy-start.5 = (bf16[24,8,256]{2,1,0:T(8,128)(2,1)S(1)}, bf16[24,8,256]{2,1,0:T(8,128)(2,1)}, u32[]{:S(2)}) copy-start(bf16[24,8,256]{2,1,0:T(8,128)(2,1)} %param.9) | copy-start | bytes 294916

commit v2 on v1

v2 whole, which is shorter than its diff:
```python
import functools

import jax
import jax.numpy as jnp
from jax import lax
from jax.experimental import pallas as pl
from jax.experimental.pallas import tpu as pltpu
from jax.sharding import PartitionSpec as P

HEADS = 8
REACH = 6
EPS = 1e-05
FLOOR = 0.5
BLOCK = 8
MESH = pl.DeviceIdType.MESH
F32 = jnp.float32
BF16 = jnp.bfloat16
OFFSETS = ((0, -1), (0, 1), (-1, 0), (1, 0), (-1, -1), (-1, 1), (1, -1), (1, 1))


def dot_nn(a, b):
    return lax.dot_general(a, b, (((1,), (0,)), ((), ())), preferred_element_type=F32)


def dot_nt(a, b):
    return lax.dot_general(a, b, (((1,), (1,)), ((), ())), preferred_element_type=F32)


def dot_tn(a, b):
    return lax.dot_general(a, b, (((0,), (0,)), ((), ())), preferred_element_type=F32)


def group_mean(x, ones):
    return dot_nn(x.astype(BF16), ones)


def kernel(
    dims,
    tok_in, cot_in, wq_in, wk_in, wv_in, wo_in, gain_in, scale,
    out, gtok, fin_out, small_out,
    tok, cot, wq, wk, wv, wo, gain,
    win, kbuf, vbuf, kraw, kinv, xhat, nrm, qu, qraw, qinv, ag, qe, ge, sc, dp, pb, db, dk, dv, dq, att,
    wg, ngs, ngo, rback, rcore, s1, rlat, s2, rz, fin, small, smcore, smlat, smz,
    load_sem, hs, hr, bs, br, cs, cr, ls, lr, zs, zr, gs, gr, ts, tr,
):
    n_lat, n_lon, rows, cols = dims
    nz = n_lon // 2
    count = rows * cols
    halo = REACH * cols
    tall = count + 2 * halo
    feats = tok_in.shape[1]
    head = feats // HEADS
    nb = BLOCK * cols
    wrows = (BLOCK + 2 * REACH) * cols
    keys = 3 * wrows
    reduce_here = 2 * feats % (2 * n_lat * nz * 16) == 0
    a = lax.axis_index("lat")
    b = lax.axis_index("lon")
    core = lax.rem(b, 2)
    z = b // 2
    sibling = (a, b + 1 - 2 * core)

    def lat_peer(j):
        return (lax.rem(a + j, n_lat), b)

    def z_peer(j):
        return (a, lax.rem(z + j, nz) * 2 + core)

    def near(da, db):
        return (lax.rem(a + da + n_lat, n_lat), lax.rem(b + db + n_lon, n_lon))

    peers = [near(*o) for o in OFFSETS]
    if reduce_here:
        peers += [sibling] + [lat_peer(j) for j in range(1, n_lat)] + [z_peer(j) for j in range(1, nz)]
    barrier = pltpu.get_barrier_semaphore()
    for p in peers:
        pl.semaphore_signal(barrier, inc=1, device_id=p, device_id_type=MESH)
    loads = []
    for src, dst in (
        (tok_in, tok), (wk_in, wk), (wv_in, wv), (gain_in, gain), (wq_in, wq), (cot_in, cot), (wo_in, wo)
    ):
        c = pltpu.make_async_copy(src, dst, load_sem.at[len(loads)])
        c.start()
        loads.append(c)
    pl.semaphore_wait(barrier, len(peers))

    def send(src, dst, s, r, to):
        c = pltpu.make_async_remote_copy(
            src_ref=src, dst_ref=dst, send_sem=s, recv_sem=r, device_id=to, device_id_type=MESH
        )
        c.start()
        return c

    def strip(da):
        return {0: (0, halo, count), 1: (count - halo, 0, halo), -1: (0, halo + count, halo)}[da]

    halos = []
    for i, (da, d) in enumerate(OFFSETS):
        src, dst, n = strip(da)
        halos.append(
            send(
                tok_in.at[pl.ds(src, n)], win.at[pl.ds((1 - d) * tall + dst, n)],
                hs.at[i], hr.at[i], near(da, d),
            )
        )

    lane = lax.broadcasted_iota(jnp.int32, (1, feats), 1) // head
    gi = lax.broadcasted_iota(jnp.int32, (feats, feats), 0) // head
    gj = lax.broadcasted_iota(jnp.int32, (feats, feats), 1) // head
    ones = jnp.where(gi == gj, 1.0 / head, 0.0).astype(BF16)

    def norm_parts(x):
        x = x.astype(F32)
        sh = x - jnp.mean(x, axis=-1, keepdims=True)
        rstd = lax.rsqrt(jnp.mean(sh * sh, axis=-1, keepdims=True) + EPS)
        return sh, rstd

    def project(x, lo, n):
        sh, rstd = norm_parts(x)
        xh = sh * rstd
        xhat[pl.ds(lo, n)] = xh
        nn = (gain[...] * xh).astype(BF16)
        nrm[pl.ds(lo, n)] = nn
        kr = dot_nn(nn, wk[...])
        kraw[pl.ds(lo, n)] = kr
        inv = lax.rsqrt(group_mean(kr * kr, ones) + FLOOR)
        kinv[pl.ds(lo, n)] = inv
        kbuf[pl.ds(lo, n)] = (kr * inv).astype(BF16)
        vbuf[pl.ds(lo, n)] = dot_nn(nn, wv[...]).astype(BF16)

    mine = tall + halo
    wide = jnp.zeros((1, feats), F32)
    for h in range(HEADS):
        wide = jnp.where(lane == h, scale[h] * (1.0 / head), wide)
    for c in loads:
        c.wait()
    project(tok[...], mine, count)
    qr = dot_nn(nrm[pl.ds(mine, count)], wq[...])
    qraw[...] = qr
    inv = lax.rsqrt(group_mean(qr * qr, ones) + FLOOR)
    qinv[...] = inv
    qu[...] = (qr * inv).astype(BF16)
    ag[...] = dot_nt(cot[...], wo[...]).astype(BF16)
    dk[...] = jnp.zeros_like(dk)
    dv[...] = jnp.zeros_like(dv)
    small[...] = jnp.zeros_like(small)
    for c in halos:
        c.wait()
    project(win[pl.ds(0, tall)], 0, tall)
    project(win[pl.ds(2 * tall, tall)], 2 * tall, tall)
    project(win[pl.ds(tall, halo)], tall, halo)
    project(win[pl.ds(tall + halo + count, halo)], tall + halo + count, halo)

    total_rows = n_lat * rows
    qi = lax.broadcasted_iota(jnp.int32, (nb, keys), 0)
    ki = lax.broadcasted_iota(jnp.int32, (nb, keys), 1)
    tile = (ki >= wrows).astype(jnp.int32) + (ki >= 2 * wrows).astype(jnp.int32)
    within = ki - tile * wrows
    row_gap = within // cols - REACH - qi // cols
    col_gap = lax.rem(within, cols) + tile * cols - cols - lax.rem(qi, cols)
    close = (jnp.abs(row_gap) <= REACH) & (jnp.abs(col_gap) <= REACH)
    krow = within // cols - REACH + a * rows

    def block(i, carried):
        q0 = pl.multiple_of(i * nb, nb)
        qb = qu[pl.ds(q0, nb)]
        gb = ag[pl.ds(q0, nb)]
        for h in range(HEADS):
            qe[pl.ds(h * nb, nb)] = jnp.where(lane == h, qb, jnp.zeros_like(qb))
            ge[pl.ds(h * nb, nb)] = jnp.where(lane == h, gb, jnp.zeros_like(gb))
        starts = [pl.multiple_of(t * tall + i * nb, 16) for t in range(3)]
        kw = jnp.concatenate([kbuf[pl.ds(s, wrows)] for s in starts], axis=0)
        vw = jnp.concatenate([vbuf[pl.ds(s, wrows)] for s in starts], axis=0)
        sc[...] = dot_nt(qe[...], kw)
        dp[...] = dot_nt(ge[...], vw)
        gr_row = krow + i * BLOCK
        seen = jnp.where(close & (gr_row >= 0) & (gr_row < total_rows), 1.0, 0.0)
        for h in range(HEADS):
            part = pl.ds(h * nb, nb)
            s = sc[part]
            e = jnp.exp(s * (scale[h] * (1.0 / head))) * seen
            p = e * (1.0 / jnp.sum(e, axis=1, keepdims=True))
            pb[part] = p.astype(BF16)
            t = dp[part]
            g = p * (t - jnp.sum(p * t, axis=1, keepdims=True))
            db[part] = g.astype(BF16)
            tot = jnp.sum(jnp.sum(g * s, axis=1, keepdims=True), axis=0, keepdims=True)
            small[1:2, :] = small[1:2, :] + jnp.where(lane == h, tot * (1.0 / head), 0.0)
        o = dot_nn(pb[...], vw)
        u = dot_nn(db[...], kw)
        oa = jnp.zeros((nb, feats), F32)
        ua = jnp.zeros((nb, feats), F32)
        for h in range(HEADS):
            oa = jnp.where(lane == h, o[h * nb : (h + 1) * nb], oa)
            ua = jnp.where(lane == h, u[h * nb : (h + 1) * nb], ua)
        att[pl.ds(q0, nb)] = oa.astype(BF16)
        dq[pl.ds(q0, nb)] = ua
        kg = dot_tn(db[...], qe[...])
        vg = dot_tn(pb[...], ge[...])
        for t in range(3):
            part = pl.ds(starts[t], wrows)
            dk[part] = dk[part] + kg[t * wrows : (t + 1) * wrows]
            dv[part] = dv[part] + vg[t * wrows : (t + 1) * wrows]
        return carried

    lax.fori_loop(0, rows // BLOCK, block, 0)

    def head_back(raw, inv, g):
        return inv * (g - raw * (inv * inv) * group_mean(g * raw, ones))

    half, quarter, last = wg.shape[1] // 2, rlat.shape[2], rz.shape[2]
    chunks = range(wg.shape[0])
    my_half = pl.multiple_of(core * half, 16)
    block_lo = pl.multiple_of(my_half + a * quarter, 16)
    leaf_lo = pl.multiple_of(block_lo + z * last, 16)

    def core_send(k):
        lo = pl.multiple_of((1 - core) * half, 16)
        return send(wg.at[k, pl.ds(lo, half)], rcore.at[k], cs.at[k], cr.at[k], sibling)

    def lat_send(k):
        s1[k] = (wg[k, pl.ds(my_half, half)].astype(F32) + rcore[k].astype(F32)).astype(BF16)
        sent = []
        for j in range(1, n_lat):
            to = lat_peer(j)
            lo = pl.multiple_of(to[0] * quarter, 16)
            sent.append(
                send(s1.at[k, pl.ds(lo, quarter)], rlat.at[k, j - 1], ls.at[k, j], lr.at[k, j], to)
            )
        return sent

    def z_send(k):
        acc = s1[k, pl.ds(pl.multiple_of(a * quarter, 16), quarter)].astype(F32)
        for j in range(1, n_lat):
            acc = acc + rlat[k, j - 1].astype(F32)
        s2[k] = acc.astype(BF16)
        sent = []
        for j in range(1, nz):
            to = z_peer(j)
            lo = pl.multiple_of((to[1] // 2) * last, 16)
            sent.append(send(s2.at[k, pl.ds(lo, last)], rz.at[k, j - 1], zs.at[k, j], zr.at[k, j], to))
        return sent

    def z_spread(k):
        acc = s2[k, pl.ds(pl.multiple_of(z * last, 16), last)].astype(F32)
        for j in range(1, nz):
            acc = acc + rz[k, j - 1].astype(F32)
        leaf = pl.ds(leaf_lo, last)
        fin[k, leaf] = acc.astype(BF16)
        return [
            send(fin.at[k, leaf], fin.at[k, leaf], gs.at[k, j], gr.at[k, j], z_peer(j))
            for j in range(1, nz)
        ]

    def lat_spread(k):
        mid = pl.ds(block_lo, quarter)
        return [
            send(fin.at[k, mid], fin.at[k, mid], gs.at[k, nz + j], gr.at[k, nz + j], lat_peer(j))
            for j in range(1, n_lat)
        ]

    def core_spread(k):
        top = pl.ds(my_half, half)
        return [send(fin.at[k, top], fin.at[k, top], gs.at[k, 0], gr.at[k, 0], sibling)]

    def done(copies):
        for c in copies:
            c.wait()

    dqr = head_back(qraw[...], qinv[...], dq[...] * wide).astype(BF16)
    wg[0, pl.ds(0, feats)] = dot_tn(nrm[pl.ds(mine, count)], dqr).astype(BF16)
    wg[0, pl.ds(feats, feats)] = dot_tn(att[...], cot[...]).astype(BF16)
    if reduce_here:
        c0 = [core_send(0)]
    dkr = head_back(kraw[...], kinv[...], dk[...] * wide).astype(BF16)
    dvb = dv[...].astype(BF16)
    wg[1, pl.ds(0, feats)] = dot_tn(nrm[...], dkr).astype(BF16)
    wg[1, pl.ds(feats, feats)] = dot_tn(nrm[...], dvb).astype(BF16)
    if reduce_here:
        c1 = [core_send(1)]
        done(c0)
        c0 = lat_send(0)
    ng = dot_nt(dkr, wk[...]) + dot_nt(dvb, wv[...])
    ngs[...] = ng.astype(BF16)
    backs = []
    for i, (da, d) in enumerate(OFFSETS):
        _, _, n = strip(da)
        src = {0: halo, -1: 0, 1: halo + count}[da]
        backs.append(
            send(
                ngs.at[pl.ds((1 + d) * tall + src, n)], rback.at[i, pl.ds(0, n)],
                bs.at[i], br.at[i], near(da, d),
            )
        )
    if reduce_here:
        done(c1)
        c1 = lat_send(1)
    from_q = dot_nt(dqr, wq[...])
    ngo[...] = ng[mine : mine + count] + from_q
    own_hat = xhat[pl.ds(mine, count)]
    small[0:1, :] = jnp.sum(ng * xhat[...], axis=0, keepdims=True) + jnp.sum(
        from_q * own_hat, axis=0, keepdims=True
    )
    if reduce_here:
        m = [send(small, smcore, ts.at[0], tr.at[0], sibling)]
        done(c0)
        c0 = z_send(0)
        done(m)
        smlat[pl.ds(a, 1)] = (small[...] + smcore[...])[None]
        m = [send(smlat.at[a], smlat.at[a], ts.at[j], tr.at[j], lat_peer(j)) for j in range(1, n_lat)]
    out[...] = (tok[...].astype(F32) + dot_nn(att[...], wo[...])).astype(BF16)
    if reduce_here:
        done(c1)
        c1 = z_send(1)
        done(c0)
        c0 = z_spread(0)
        done(m)
        acc = smlat[0]
        for j in range(1, n_lat):
            acc = acc + smlat[j]
        smz[pl.ds(z, 1)] = acc[None]
        m = [
            send(smz.at[z], smz.at[z], ts.at[n_lat + j], tr.at[n_lat + j], z_peer(j))
            for j in range(1, nz)
        ]
        done(c1)
        c1 = z_spread(1)
        done(c0)
        c0 = lat_spread(0)
        done(c1)
        c1 = lat_spread(1)
    done(backs)
    ngo[...] = ngo[...] + rback[0].astype(F32) + rback[1].astype(F32)
    for da, lo in ((-1, 0), (1, count - halo)):
        part = pl.ds(lo, halo)
        add = ngo[part]
        for i, o in enumerate(OFFSETS):
            if o[0] == -da:
                add = add + rback[i, pl.ds(0, halo)].astype(F32)
        ngo[part] = add
    sh, rstd = norm_parts(tok[...])
    g = ngo[...] * gain[...]
    tg = rstd * (
        g
        - jnp.mean(g, axis=-1, keepdims=True)
        - own_hat * jnp.mean(g * own_hat, axis=-1, keepdims=True)
    )
    gtok[...] = (cot[...].astype(F32) + tg).astype(BF16)
    if reduce_here:
        done(c0)
        c0 = core_spread(0)
        done(c1)
        c1 = core_spread(1)
        done(m)
        acc = smz[0]
        for j in range(1, nz):
            acc = acc + smz[j]
        small_out[...] = acc
        done(c0)
        fin_out[0] = fin[0]
        done(c1)
        fin_out[1] = fin[1]
    else:
        fin_out[...] = wg[...]
        small_out[...] = small[...]


def finish(fin, small, out, gtok, *refs):
    results, staged, sem = refs[:8], refs[8:14], refs[14]
    feats = fin.shape[2]
    pending = []

    def store(src, dst):
        c = pltpu.make_async_copy(src, dst, sem.at[len(pending)])
        c.start()
        pending.append(c)

    store(out, results[0])
    store(gtok, results[1])
    for n, (k, lo) in enumerate(((0, 0), (1, 0), (1, feats), (0, feats))):
        staged[n][...] = fin[k, pl.ds(lo, feats)].astype(F32)
        store(staged[n], results[2 + n])
    staged[4][...] = small[0:1, :]
    store(staged[4], results[6])
    lane = lax.broadcasted_iota(jnp.int32, (feats, HEADS), 0)
    col = lax.broadcasted_iota(jnp.int32, (feats, HEADS), 1)
    pick = jnp.where(lane == col * (feats // HEADS), 1.0, 0.0)
    staged[5][...] = lax.dot_general(
        small[...], pick, (((1,), (0,)), ((), ())), precision=lax.Precision.HIGHEST,
        preferred_element_type=F32,
    )[1:2, :]
    store(staged[5], results[7])
    for c in pending:
        c.wait()


def local(dims, tokens, cotangent, wq, wk, wv, wo, norm_gain, logit_scale):
    n_lat, n_lon, rows, cols = dims
    nz = n_lon // 2
    feats = tokens.shape[-1]
    head = feats // HEADS
    count = rows * cols
    halo = REACH * cols
    window = 3 * (count + 2 * halo)
    nb = BLOCK * cols * HEADS
    keys = 3 * (BLOCK + 2 * REACH) * cols
    reduce_here = 2 * feats % (2 * n_lat * nz * 16) == 0
    half = feats
    quarter = half // n_lat if reduce_here else 16
    last = quarter // nz if reduce_here else 16
    pl_lat = n_lat if reduce_here else 2
    pl_z = nz if reduce_here else 2
    vm = pl.BlockSpec(memory_space=pltpu.VMEM)
    sm = pl.BlockSpec(memory_space=pltpu.SMEM)
    hbm = pl.BlockSpec(memory_space=pltpu.HBM)
    dma = pltpu.SemaphoreType.DMA
    V = pltpu.VMEM
    square = V((feats, feats), BF16)
    scratch = [
        V((count, feats), BF16), V((count, feats), BF16), square, square, square, square,
        V((1, feats), F32),
        V((window, feats), BF16), V((window, feats), BF16), V((window, feats), BF16),
        V((window, feats), F32), V((window, feats), F32), V((window, feats), F32),
        V((window, feats), BF16),
        V((count, feats), BF16), V((count, feats), F32), V((count, feats), F32),
        V((count, feats), BF16),
        V((nb, feats), BF16), V((nb, feats), BF16),
        V((nb, keys), F32), V((nb, keys), F32), V((nb, keys), BF16), V((nb, keys), BF16),
        V((window, feats), F32), V((window, feats), F32), V((count, feats), F32),
        V((count, feats), BF16),
        V((2, 2 * feats, feats), BF16), V((window, feats), BF16), V((count, feats), F32),
        V((8, count, feats), BF16),
        V((2, half, feats), BF16), V((2, half, feats), BF16),
        V((2, pl_lat - 1, quarter, feats), BF16), V((2, quarter, feats), BF16),
        V((2, pl_z - 1, last, feats), BF16), V((2, 2 * feats, feats), BF16),
        V((8, feats), F32), V((8, feats), F32), V((pl_lat, 8, feats), F32), V((pl_z, 8, feats), F32),
        dma((7,)),
        dma((8,)), dma((8,)), dma((8,)), dma((8,)), dma((2,)), dma((2,)),
        dma((2, pl_lat)), dma((2, pl_lat)), dma((2, pl_z)), dma((2, pl_z)),
        dma((2, pl_lat + pl_z)), dma((2, pl_lat + pl_z)),
        dma((pl_lat + pl_z,)), dma((pl_lat + pl_z,)),
    ]
    out, gtok, fin, small = pl.pallas_call(
        functools.partial(kernel, dims),
        out_shape=[
            jax.ShapeDtypeStruct((count, feats), BF16),
            jax.ShapeDtypeStruct((count, feats), BF16),
            jax.ShapeDtypeStruct((2, 2 * feats, feats), BF16),
            jax.ShapeDtypeStruct((8, feats), F32),
        ],
        in_specs=[hbm] * 7 + [sm],
        out_specs=[vm] * 4,
        scratch_shapes=scratch,
        compiler_params=pltpu.CompilerParams(
            collective_id=0, has_side_effects=True, vmem_limit_bytes=60 * 1024 * 1024
        ),
    )(
        tokens.reshape(count, feats), cotangent.reshape(count, feats), wq, wk, wv, wo,
        norm_gain.reshape(1, feats), logit_scale,
    )
    if not reduce_here:
        fin, small = lax.psum((fin, small), ("lat", "lon"))
    weight = jax.ShapeDtypeStruct((feats, feats), F32)
    tile = jax.ShapeDtypeStruct((count, feats), BF16)
    done = pl.pallas_call(
        finish,
        out_shape=[
            tile, tile, weight, weight, weight, weight,
            jax.ShapeDtypeStruct((1, feats), F32), jax.ShapeDtypeStruct((1, HEADS), F32),
        ],
        in_specs=[vm] * 4,
        out_specs=[hbm] * 8,
        scratch_shapes=[V((feats, feats), F32)] * 4
        + [V((1, feats), F32), V((1, HEADS), F32), dma((8,))],
        compiler_params=pltpu.CompilerParams(vmem_limit_bytes=60 * 1024 * 1024),
    )(fin, small, out, gtok)
    return (
        done[0].reshape(rows, cols, feats), done[1].reshape(rows, cols, feats),
        *done[2:6], done[6].reshape(feats), done[7].reshape(HEADS),
    )


def solution(mesh):
    n_lat, n_lon = mesh.shape["lat"], mesh.shape["lon"]

    def run(tokens, *rest):
        dims = (n_lat, n_lon, tokens.shape[0], tokens.shape[1])
        return local(dims, tokens, *rest)

    return jax.shard_map(
        run,
        mesh=mesh,
        in_specs=(P("lat", "lon", None), P("lat", "lon", None), P(), P(), P(), P(), P(), P()),
        out_specs=(P("lat", "lon", None), P("lat", "lon", None), P(), P(), P(), P(), P(), P()),
        check_vma=False,
    )
```

time: 52.4 us -> 44.2 us (0.84)
  local copies, waits for them, and re-layouts: 10.2 us -> 0 us
  Pallas kernels: 41.2 us -> 43.4 us
    unnamed x18 -> x0, local copies, waits for them, and re-layouts: 7.93 us -> none
    pallas_call x0 -> x1, Pallas kernels: none -> 2.21 us  [local(): pl.pallas_call(finish, out_shape=[tile, tile, weight, weight, weight, wei...]
    slice x3 -> x0, local copies, waits for them, and re-layouts: 2.14 us -> none  [the longest x1 0.98 us: local(): fin[3 * feats:]]
where the time goes in v2:
time: 44.2 us; the launch traced here: 44.1 us
  Pallas kernels  43.4 us (98%)
  between operations  0.64 us (1%)
    pallas_call x1, Pallas kernels, local(): pl.pallas_call(functools.partial(kernel, dims), out_shape=[jax.ShapeDtype...  41.2 us
    pallas_call x1, Pallas kernels, local(): pl.pallas_call(finish, out_shape=[tile, tile, weight, weight, weight, wei...  2.21 us

profile of v2, /device:TPU:0, one launch (start us, length us, event | category | flops | bytes accessed | tf_op | source)
XLA Modules:
  0.0 44.1 jit_solution(4234085230832871365)
XLA Ops:
  0.6 41.2 %shard_map.143 = (bf16[192,256]{1,0:T(8,128)(2,1)}, bf16[192,256]{1,0:T(8,128)(2,1)}, bf16[2,512,256]{2,1,0:T(8,128)(2,1)}, f32[8,256]{1,0:T(8,128)}) custom-call(bf16[192,256]{1,0:T(8,128)(2,1)} %bitcast.7, bf16[192,256]{1,0:T(8,128)(2,1)} %bitcast.8, bf16[256,256]{1,0:T(8,128)(2,1)} %wq_in.1, bf16[256,256]{1,0:T(8,128)(2,1)} %wk_in.1, ...), custom_call_target="tpu_custom_call" | custom-call | tf_op jit(solution)/shard_map/pallas_call | solution.py:443
  41.8 2.2 %shard_map.144 = (bf16[192,256]{1,0:T(8,128)(2,1)}, bf16[192,256]{1,0:T(8,128)(2,1)}, f32[256,256]{1,0:T(8,128)}, f32[256,256]{1,0:T(8,128)}, f32[256,256]{1,0:T...) custom-call(bf16[2,512,256]{2,1,0:T(8,128)(2,1)} %get-tuple-element.20.fin, ...), custom_call_target="tpu_custom_call" | custom-call | tf_op jit(solution)/shard_map/pallas_call | solution.py:465

commit v3 on v2

--- a/solution.py
+++ b/solution.py
@@ -259,9 +259,17 @@
             for j in range(1, n_lat)
         ]
 
-    def core_spread(k):
-        top = pl.ds(my_half, half)
-        return [send(fin.at[k, top], fin.at[k, top], gs.at[k, 0], gr.at[k, 0], sibling)]
+    def core_spread(k, j):
+        lo = pl.multiple_of(my_half + lax.rem(a - j + n_lat, n_lat) * quarter, 16)
+        rows_j, sem = pl.ds(lo, quarter), nz + n_lat + j
+        return send(fin.at[k, rows_j], fin.at[k, rows_j], gs.at[k, sem], gr.at[k, sem], sibling)
+
+    def forward(k, copies):
+        sent = []
+        for j, c in enumerate(copies):
+            c.wait()
+            sent.append(core_spread(k, j + 1))
+        return sent
 
     def done(copies):
         for c in copies:
@@ -327,8 +335,10 @@
         c1 = z_spread(1)
         done(c0)
         c0 = lat_spread(0)
+        own0 = core_spread(0, 0)
         done(c1)
         c1 = lat_spread(1)
+        own1 = core_spread(1, 0)
     done(backs)
     ngo[...] = ngo[...] + rback[0].astype(F32) + rback[1].astype(F32)
     for da, lo in ((-1, 0), (1, count - halo)):
@@ -347,10 +357,8 @@
     )
     gtok[...] = (cot[...].astype(F32) + tg).astype(BF16)
     if reduce_here:
-        done(c0)
-        c0 = core_spread(0)
-        done(c1)
-        c1 = core_spread(1)
+        c0 = forward(0, c0) + [own0]
+        c1 = forward(1, c1) + [own1]
         done(m)
         acc = smz[0]
         for j in range(1, nz):
@@ -437,7 +445,7 @@
         dma((7,)),
         dma((8,)), dma((8,)), dma((8,)), dma((8,)), dma((2,)), dma((2,)),
         dma((2, pl_lat)), dma((2, pl_lat)), dma((2, pl_z)), dma((2, pl_z)),
-        dma((2, pl_lat + pl_z)), dma((2, pl_lat + pl_z)),
+        dma((2, 2 * pl_lat + pl_z)), dma((2, 2 * pl_lat + pl_z)),
         dma((pl_lat + pl_z,)), dma((pl_lat + pl_z,)),
     ]
     out, gtok, fin, small = pl.pallas_call(

time: 44.2 us -> 44.2 us (level)
  no operation moved by 1% of the time
where the time goes in v3:
time: 44.2 us; the launch traced here: 44.1 us
  Pallas kernels  43.4 us (98%)
  between operations  0.64 us (1%)
    pallas_call x1, Pallas kernels, local(): pl.pallas_call(functools.partial(kernel, dims), out_shape=[jax.ShapeDtype...  41.2 us
    pallas_call x1, Pallas kernels, local(): pl.pallas_call(finish, out_shape=[tile, tile, weight, weight, weight, wei...  2.21 us

profile of v3, /device:TPU:0, one launch (start us, length us, event | category | flops | bytes accessed | tf_op | source)
XLA Modules:
  0.0 44.1 jit_solution(6102966835848138863)
XLA Ops:
  0.6 41.2 %shard_map.143 = (bf16[192,256]{1,0:T(8,128)(2,1)}, bf16[192,256]{1,0:T(8,128)(2,1)}, bf16[2,512,256]{2,1,0:T(8,128)(2,1)}, f32[8,256]{1,0:T(8,128)}) custom-call(bf16[192,256]{1,0:T(8,128)(2,1)} %bitcast.7, bf16[192,256]{1,0:T(8,128)(2,1)} %bitcast.8, bf16[256,256]{1,0:T(8,128)(2,1)} %wq_in.1, bf16[256,256]{1,0:T(8,128)(2,1)} %wk_in.1, ...), custom_call_target="tpu_custom_call" | custom-call | tf_op jit(solution)/shard_map/pallas_call | solution.py:451
  41.9 2.2 %shard_map.144 = (bf16[192,256]{1,0:T(8,128)(2,1)}, bf16[192,256]{1,0:T(8,128)(2,1)}, f32[256,256]{1,0:T(8,128)}, f32[256,256]{1,0:T(8,128)}, f32[256,256]{1,0:T...) custom-call(bf16[2,512,256]{2,1,0:T(8,128)(2,1)} %get-tuple-element.20.fin, ...), custom_call_target="tpu_custom_call" | custom-call | tf_op jit(solution)/shard_map/pallas_call | solution.py:473
